TPU v7x, 128 devices: a whole 4x4x4 slice. The times are simulated.
128 devices in a mesh: section: 2 (over x_hi), dp: 32 (over x_lo, y, z), tensor: 2 (over core).
Axes of the slice: x: 4 (x_hi: 2, x_lo: 2; x = x_hi * 2 + x_lo), y: 4, z: 4, core: 2. Of those that a mesh axis runs over, the one named last changes fastest.
Arguments:
- inputs: bfloat16 [32, 2, 128, 1536], P('dp', None, 'tensor'), may hold values from -6 to 6
- out_cotangent: bfloat16 [32, 2, 128, 1536], P('dp', None, 'tensor'), may hold values from -6 to 6
- segments: int32 [32, 2, 128], P('dp'), may hold values from 0 to 2, as said below
- norm_gains: bfloat16 [2, 2, 1536], replicated, may hold values from 0.25 to 1.75
- conv_kernel: bfloat16 [3, 1536], replicated, may hold values from -3 to 3
- qk_gains: bfloat16 [2, 64], replicated, may hold values from 0.25 to 1.75
- conv_in: bfloat16 [1536, 3, 1536], P(('section', 'dp'), None, 'tensor'), may hold values from -0.15625 to 0.15625
- attn_qkv: bfloat16 [1536, 2560], P(('section', 'dp'), 'tensor'), may hold values from -0.15625 to 0.15625
- mixer_out: bfloat16 [2, 1536, 1536], P('section', 'tensor'), may hold values from -0.3125 to 0.3125
- gate_up: bfloat16 [2, 2, 1536, 6912], P('section', None, None, 'tensor'), may hold values from -0.15625 to 0.15625
- down: bfloat16 [2, 6912, 1536], P('section', 'tensor'), may hold values from -0.078125 to 0.078125
Outputs:
- activations: bfloat16 [2, 32, 2, 128, 1536], P('section', 'dp', None, 'tensor')
- input_grads: bfloat16 [2, 32, 2, 128, 1536], P('section', 'dp', None, 'tensor')
- grad_norm_gains: float32 [2, 2, 1536], replicated
- grad_conv_kernel: float32 [3, 1536], replicated
- grad_qk_gains: float32 [2, 64], replicated
- grad_conv_in: float32 [1536, 3, 1536], P(('section', 'dp'), None, 'tensor')
- grad_attn_qkv: float32 [1536, 2560], P(('section', 'dp'), 'tensor')
- grad_mixer_out: float32 [2, 1536, 1536], P('section', 'tensor', 'dp')
- grad_gate_up: float32 [2, 2, 1536, 6912], P('section', None, 'dp', 'tensor')
- grad_down: float32 [2, 6912, 1536], P('section', 'tensor', 'dp')
Inputs may be any that keep to these rules, and one draw needn't show every extreme that they name: `segments`: segment numbers never fall along a sequence, and every document has 16 positions or more.
All inputs are finite; a program needn't handle non-finite values.
Results may differ from a plain program's by a relative error of at most 0.04.
Values may be sent and summed in bfloat16 or wider, within the bound.
No kernel may reach another device: no remote copies, remote signals or barrier semaphores. Data moves between devices by JAX's collectives and lax.ppermute only.
A program may use at most 448 MiB of HBM per device.

v0:
```python
import math

import jax
import jax.numpy as jnp
from jax import lax
from jax.sharding import PartitionSpec as P

HEADS = 24
KV_HEADS = 8
HEAD_DIM = 64


EPSILON = 1e-05
ROPE_BASE = 1000000.0
MASKED_SCORE = -1e30


def joined_along(tiles, dim):
    lengths = list(tiles.shape[1:])
    lengths[dim] *= tiles.shape[0]
    return jnp.moveaxis(tiles, 0, dim).reshape(lengths)


def from_everyone(shard, axis):
    copies = jnp.broadcast_to(shard, (lax.axis_size(axis), *shard.shape))
    return lax.all_to_all(copies, axis, split_axis=0, concat_axis=0, tiled=True)


def gathered_copies(shard, axis, dim):
    return joined_along(from_everyone(shard, axis), dim)


def cut_along(shard, dim, length):
    lengths = shard.shape
    tiles = shard.reshape(*lengths[:dim], length, lengths[dim] // length, *lengths[dim + 1 :])
    return jnp.moveaxis(tiles, dim, 0)


def sent_and_summed(shard, axis, dim):
    tiles = cut_along(shard, dim, lax.axis_size(axis))
    arrived = lax.all_to_all(tiles, axis, split_axis=0, concat_axis=0, tiled=True)
    return arrived.astype(jnp.float32).sum(axis=0)


def as_sent(shard):
    return jax.tree.map(lambda a: a.astype(jnp.bfloat16) if a.dtype == jnp.float32 else a, shard)


def sent_together(arrays, axis, dim, along):
    widths = [math.prod(a.shape[along:]) for a in arrays]
    both = jnp.concatenate(
        [a.reshape(*a.shape[:along], w) for a, w in zip(arrays, widths)], axis=along
    )
    whole = lax.all_gather(both, axis, axis=dim, tiled=True)
    tiles = jnp.split(whole, [sum(widths[:k]) for k in range(1, len(widths))], axis=along)
    return tuple((b.reshape(*whole.shape[:along], *a.shape[along:]) for a, b in zip(arrays, tiles)))


def passed_along(shard, axis, by):
    length = lax.axis_size(axis)
    pairs = [(i, i + by) for i in range(length) if 0 <= i + by < length]
    return lax.ppermute(shard, axis, pairs)


def sum_packed(arrays, axis, dims):
    length = lax.axis_size(axis)
    tiles = [cut_along(a, dim, length) for a, dim in zip(arrays, dims)]
    lines = jnp.concatenate([b.reshape(length, -1) for b in tiles], axis=1)
    span = max(16, -(-lines.shape[1] // 1024) * 8)
    lines = jnp.pad(lines, ((0, 0), (0, span * 128 - lines.shape[1]))).reshape(-1, 128)
    ravelled, at, finished = (lax.psum_scatter(lines, axis, tiled=True).reshape(-1), 0, [])
    for b in tiles:
        part = b[0]
        finished.append(ravelled[at : at + part.size].reshape(part.shape))
        at += part.size
    return tuple(finished)


def over_pieces(shard, axis):
    return lax.all_gather(shard, axis).sum(0)


def spread(piece):
    return gathered_copies(piece, "tensor", 0)


def collect(partial_sum):
    return jax.tree.map(lambda part: sent_and_summed(part, "tensor", 0), as_sent(partial_sum))


def product(left, right):
    return jnp.dot(left, right, preferred_element_type=jnp.float32)


def product_left(left, right):
    return lax.dot_general(
        left, right, (((0,), (0,)), ((), ())), preferred_element_type=jnp.float32
    )


def product_right(left, right):
    return lax.dot_general(
        left, right, (((1,), (1,)), ((), ())), preferred_element_type=jnp.float32
    )


def normalize(values):
    return values * lax.rsqrt(jnp.mean(values * values, axis=-1, keepdims=True) + EPSILON)


def norm_backward(grad_normed, values, normed):
    inverse_rms = lax.rsqrt(jnp.mean(values * values, axis=-1, keepdims=True) + EPSILON)
    return inverse_rms * (
        grad_normed - normed * jnp.mean(grad_normed * normed, axis=-1, keepdims=True)
    )


def shift_rows(values, offset):
    return jnp.concatenate(
        [jnp.zeros((offset, values.shape[1]), values.dtype), values[:-offset]], axis=0
    )


def conv_gate(projected, kernel, segment_ids):
    channels = kernel.shape[1]
    taps = kernel.shape[0]
    gate_before = projected[:, :channels]
    gate_after = projected[:, channels : 2 * channels]
    signal = projected[:, 2 * channels :]
    mixed = gate_before * signal
    total = kernel[taps - 1] * mixed
    for offset in range(1, taps):
        same_doc = (segment_ids[offset:] == segment_ids[:-offset]).astype(mixed.dtype)
        same_doc = jnp.concatenate([jnp.zeros((offset,), mixed.dtype), same_doc])
        total = total + kernel[taps - 1 - offset] * shift_rows(mixed, offset) * same_doc[:, None]
    return gate_after * total


def rotary_tables(length, head_size):
    half_size = head_size // 2
    exponent = jnp.arange(half_size, dtype=jnp.float32) * (2.0 / head_size)
    frequency = jnp.exp(-exponent * jnp.log(ROPE_BASE))
    angles = jnp.arange(length, dtype=jnp.float32)[:, None] * frequency[None, :]
    return (jnp.cos(angles), jnp.sin(angles))


def rotate(values, cosine_table, sine_table):
    half_size = values.shape[-1] // 2
    first_half = values[..., :half_size]
    second_half = values[..., half_size:]
    shape_out = (cosine_table.shape[0],) + (1,) * (values.ndim - 2) + (half_size,)
    cosine_table = cosine_table.reshape(shape_out)
    sine_table = sine_table.reshape(shape_out)
    return jnp.concatenate(
        [
            first_half * cosine_table - second_half * sine_table,
            second_half * cosine_table + first_half * sine_table,
        ],
        axis=-1,
    )


def prepare_heads(head_inputs, head_gains):
    length = head_inputs.shape[0]
    group_size = HEADS // KV_HEADS
    key_heads = head_inputs.shape[1] // ((group_size + 2) * HEAD_DIM)
    grouped = head_inputs.reshape(length, key_heads, group_size + 2, HEAD_DIM)
    cosine_table, sine_table = rotary_tables(length, HEAD_DIM)
    queries = rotate(
        normalize(grouped[:, :, :group_size]) * head_gains[0], cosine_table, sine_table
    )
    keys_out = rotate(
        normalize(grouped[:, :, group_size]) * head_gains[1], cosine_table, sine_table
    )
    return (queries, keys_out, grouped[:, :, group_size + 1])


def head_scores(queries_low, keys_low, segment_ids):
    length = segment_ids.shape[0]
    scores = jnp.einsum(
        "tgjd,sgd->gjts", queries_low, keys_low, preferred_element_type=jnp.float32
    ) * HEAD_DIM ** (-0.5)
    position = jnp.arange(length)
    allowed = (position[:, None] >= position[None, :]) & (
        segment_ids[:, None] == segment_ids[None, :]
    )
    return jnp.where(allowed, scores, MASKED_SCORE)


def score_shape(length, weight_qkv):
    group_size = HEADS // KV_HEADS
    key_heads = weight_qkv.shape[1] // ((group_size + 2) * HEAD_DIM)
    return (key_heads, group_size, length, 1)


def conv_forward(operands):
    normed_full, segment_ids, weight_in, kernel, weight_qkv, head_gains, weight_out = operands
    length = normed_full.shape[0]
    projected = product(normed_full, weight_in)
    gated_low = conv_gate(projected, kernel, segment_ids).astype(jnp.bfloat16)
    return (
        gated_low,
        product(gated_low, weight_out),
        projected,
        jnp.zeros((length, weight_qkv.shape[1]), jnp.float32),
        jnp.zeros(score_shape(length, weight_qkv), jnp.float32),
    )


def attention_forward(operands):
    normed_full, segment_ids, weight_in, kernel, weight_qkv, head_gains, weight_out = operands
    length = normed_full.shape[0]
    head_inputs = product(normed_full, weight_qkv)
    queries, keys_out, values_out = prepare_heads(head_inputs, head_gains)
    queries_low = queries.astype(jnp.bfloat16)
    keys_low = keys_out.astype(jnp.bfloat16)
    values_low = values_out.astype(jnp.bfloat16)
    scores = head_scores(queries_low, keys_low, segment_ids)
    row_max = jnp.max(scores, axis=-1, keepdims=True)
    log_total = row_max + jnp.log(jnp.sum(jnp.exp(scores - row_max), axis=-1, keepdims=True))
    weights_low = jnp.exp(scores - log_total).astype(jnp.bfloat16)
    attended = jnp.einsum(
        "gjts,sgd->tgjd", weights_low, values_low, preferred_element_type=jnp.float32
    )
    gated_low = attended.reshape(length, -1).astype(jnp.bfloat16)
    return (
        gated_low,
        product(gated_low, weight_out),
        jnp.zeros((length, weight_in.shape[1]), jnp.float32),
        head_inputs,
        log_total,
    )


def spare_forward(operands):
    normed_full, segment_ids, weight_in, kernel, weight_qkv, head_gains, weight_out = operands
    length = normed_full.shape[0]
    return (
        jnp.zeros((length, weight_out.shape[0]), jnp.bfloat16),
        jnp.zeros((length, weight_out.shape[1]), jnp.float32),
        jnp.zeros((length, weight_in.shape[1]), jnp.float32),
        jnp.zeros((length, weight_qkv.shape[1]), jnp.float32),
        jnp.zeros(score_shape(length, weight_qkv), jnp.float32),
    )


def conv_backward(operands):
    (
        normed_full,
        segment_ids,
        weight_in,
        kernel,
        weight_qkv,
        head_gains,
        weight_out,
        gated_low,
        projected,
        head_inputs,
        log_total,
        grad_mix_full,
    ) = operands
    length = normed_full.shape[0]
    grad_gated = product_right(grad_mix_full, weight_out)
    rebuild = jax.vjp(
        lambda proj_in, kern_in: conv_gate(proj_in, kern_in, segment_ids), projected, kernel
    )[1]
    grad_proj, grad_kernel = rebuild(grad_gated)
    grad_low = grad_proj.astype(jnp.bfloat16)
    return (
        product_right(grad_low, weight_in),
        grad_low,
        jnp.zeros((length, weight_qkv.shape[1]), jnp.bfloat16),
        grad_kernel,
        jnp.zeros(head_gains.shape, jnp.float32),
    )


def attention_backward(operands):
    (
        normed_full,
        segment_ids,
        weight_in,
        kernel,
        weight_qkv,
        head_gains,
        weight_out,
        gated_low,
        projected,
        head_inputs,
        log_total,
        grad_mix_full,
    ) = operands
    length = normed_full.shape[0]
    grad_attended = product_right(grad_mix_full, weight_out)
    prepared, rebuild = jax.vjp(prepare_heads, head_inputs, head_gains)
    queries, keys_out, values_out = prepared
    queries_low = queries.astype(jnp.bfloat16)
    keys_low = keys_out.astype(jnp.bfloat16)
    values_low = values_out.astype(jnp.bfloat16)
    scores = head_scores(queries_low, keys_low, segment_ids)
    weights = jnp.exp(scores - log_total)
    weights_low = weights.astype(jnp.bfloat16)
    grad_low = grad_attended.reshape(queries.shape).astype(jnp.bfloat16)
    grad_values = jnp.einsum(
        "gjts,tgjd->sgd", weights_low, grad_low, preferred_element_type=jnp.float32
    )
    grad_weights = jnp.einsum(
        "tgjd,sgd->gjts", grad_low, values_low, preferred_element_type=jnp.float32
    )
    grad_scores = (
        weights * (grad_weights - jnp.sum(grad_weights * weights, axis=-1, keepdims=True))
    ).astype(jnp.bfloat16)
    scale_factor = HEAD_DIM ** (-0.5)
    grad_queries = (
        jnp.einsum("gjts,sgd->tgjd", grad_scores, keys_low, preferred_element_type=jnp.float32)
        * scale_factor
    )
    grad_keys = (
        jnp.einsum("gjts,tgjd->sgd", grad_scores, queries_low, preferred_element_type=jnp.float32)
        * scale_factor
    )
    grad_inputs, grad_heads = rebuild((grad_queries, grad_keys, grad_values))
    grad_inputs_low = grad_inputs.astype(jnp.bfloat16)
    return (
        product_right(grad_inputs_low, weight_qkv),
        jnp.zeros((length, weight_in.shape[1]), jnp.bfloat16),
        grad_inputs_low,
        jnp.zeros(kernel.shape, jnp.float32),
        grad_heads,
    )


def spare_backward(operands):
    (
        normed_full,
        segment_ids,
        weight_in,
        kernel,
        weight_qkv,
        head_gains,
        weight_out,
        gated_low,
        projected,
        head_inputs,
        log_total,
        grad_mix_full,
    ) = operands
    length = normed_full.shape[0]
    return (
        jnp.zeros(normed_full.shape, jnp.float32),
        jnp.zeros((length, weight_in.shape[1]), jnp.bfloat16),
        jnp.zeros((length, weight_qkv.shape[1]), jnp.bfloat16),
        jnp.zeros(kernel.shape, jnp.float32),
        jnp.zeros(head_gains.shape, jnp.float32),
    )


def ffn_forward(operands):
    inner_full, weight_gate, weight_up, weight_down = operands
    gate_value = product(inner_full, weight_gate)
    up_value = product(inner_full, weight_up)
    active_low = (jax.nn.silu(gate_value) * up_value).astype(jnp.bfloat16)
    return (gate_value, up_value, active_low, product(active_low, weight_down))


def ffn_spare(operands):
    inner_full, weight_gate, weight_up, weight_down = operands
    length = inner_full.shape[0]
    hidden_units = weight_gate.shape[1]
    return (
        jnp.zeros((length, hidden_units), jnp.float32),
        jnp.zeros((length, hidden_units), jnp.float32),
        jnp.zeros((length, hidden_units), jnp.bfloat16),
        jnp.zeros((length, weight_down.shape[1]), jnp.float32),
    )


def ffn_backward(operands):
    inner_full, weight_gate, weight_up, weight_down, gate_value, up_value, active_low, grad_full = (
        operands
    )
    grad_active = product_right(grad_full, weight_down)
    sigmoid_gate = jax.nn.sigmoid(gate_value)
    grad_gate = (
        grad_active * up_value * sigmoid_gate * (1.0 + gate_value * (1.0 - sigmoid_gate))
    ).astype(jnp.bfloat16)
    grad_up = (grad_active * gate_value * sigmoid_gate).astype(jnp.bfloat16)
    grad_inner = product_right(grad_gate, weight_gate) + product_right(grad_up, weight_up)
    return (grad_inner, jnp.stack([grad_gate, grad_up], axis=1))


def ffn_back_spare(operands):
    inner_full, weight_gate, weight_up, weight_down, gate_value, up_value, active_low, grad_full = (
        operands
    )
    length = inner_full.shape[0]
    return (
        jnp.zeros(inner_full.shape, jnp.float32),
        jnp.zeros((length, 2, weight_gate.shape[1]), jnp.bfloat16),
    )


def layer_forward(layer_in, norm_scale, segment_ids, branch_index, in_range, weights):
    weight_in, kernel, weight_qkv, head_gains, weight_out, weight_gate, weight_up, weight_down = (
        weights
    )
    normed_full = spread((normalize(layer_in) * norm_scale[0]).astype(jnp.bfloat16))
    gated_low, mixer_part, projected, head_inputs, log_total = lax.switch(
        branch_index,
        [conv_forward, attention_forward, spare_forward],
        (normed_full, segment_ids, weight_in, kernel, weight_qkv, head_gains, weight_out),
    )
    hidden = layer_in + collect(mixer_part)
    inner_full = spread((normalize(hidden) * norm_scale[1]).astype(jnp.bfloat16))
    gate_value, up_value, active_low, ffn_part = lax.cond(
        in_range, ffn_forward, ffn_spare, (inner_full, weight_gate, weight_up, weight_down)
    )
    result = hidden + collect(ffn_part)
    return (
        result,
        (
            layer_in,
            normed_full,
            gated_low,
            projected,
            head_inputs,
            log_total,
            hidden,
            inner_full,
            gate_value,
            up_value,
            active_low,
        ),
    )


def layer_backward(grad_result, saved, norm_scale, segment_ids, branch_index, in_range, weights):
    weight_in, kernel, weight_qkv, head_gains, weight_out, weight_gate, weight_up, weight_down = (
        weights
    )
    (
        layer_in,
        normed_full,
        gated_low,
        projected,
        head_inputs,
        log_total,
        hidden,
        inner_full,
        gate_value,
        up_value,
        active_low,
    ) = saved
    grad_full = spread(grad_result.astype(jnp.bfloat16))
    grad_inner_part, grad_pair = lax.cond(
        in_range,
        ffn_backward,
        ffn_back_spare,
        (
            inner_full,
            weight_gate,
            weight_up,
            weight_down,
            gate_value,
            up_value,
            active_low,
            grad_full,
        ),
    )
    grad_inner = collect(grad_inner_part)
    inner_normed = normalize(hidden)
    grad_scale_inner = jnp.sum(grad_inner * inner_normed, axis=0)
    grad_hidden = grad_result + norm_backward(grad_inner * norm_scale[1], hidden, inner_normed)
    grad_mix_full = spread(grad_hidden.astype(jnp.bfloat16))
    grad_normed_part, grad_in_low, grad_qkv_low, grad_kernel, grad_heads = lax.switch(
        branch_index,
        [conv_backward, attention_backward, spare_backward],
        (
            normed_full,
            segment_ids,
            weight_in,
            kernel,
            weight_qkv,
            head_gains,
            weight_out,
            gated_low,
            projected,
            head_inputs,
            log_total,
            grad_mix_full,
        ),
    )
    grad_normed = collect(grad_normed_part)
    outer_normed = normalize(layer_in)
    grad_scale_outer = jnp.sum(grad_normed * outer_normed, axis=0)
    grad_layer_in = grad_hidden + norm_backward(grad_normed * norm_scale[0], layer_in, outer_normed)
    section_rows = (gated_low, grad_mix_full, inner_full, grad_pair, active_low, grad_full)
    mixer_rows = (normed_full, grad_in_low, grad_qkv_low)
    return (
        grad_layer_in,
        section_rows,
        mixer_rows,
        (jnp.stack([grad_scale_outer, grad_scale_inner]), grad_kernel, grad_heads),
    )


def join_rows(rows_list, count):
    return [jnp.concatenate([rows[index] for rows in rows_list], axis=0) for index in range(count)]


def section_grads(rows_list):
    gated_rows, grad_mix_rows, inner_rows, pair_rows, active_rows, grad_rows = join_rows(
        rows_list, 6
    )
    grad_out_w = product_left(gated_rows, grad_mix_rows)[None]
    grad_pair_w = jnp.einsum(
        "td,tkf->kdf", inner_rows, pair_rows, preferred_element_type=jnp.float32
    )[None]
    grad_down_w = product_left(active_rows, grad_rows)[None]
    return (grad_out_w, grad_pair_w, grad_down_w)


def accumulate(totals, update):
    if totals is None:
        return update
    return jax.tree.map(jnp.add, totals, update)


def local(
    inputs,
    out_cotangent,
    segments,
    norm_gains,
    conv_kernel,
    qk_gains,
    conv_in,
    attn_qkv,
    mixer_out,
    gate_up,
    down,
):
    section_index = lax.axis_index("section")
    first_section = section_index == 0
    tensor_rank = lax.axis_index("tensor")
    channels = conv_in.shape[2]
    micro_count = inputs.shape[1]
    kernel = lax.dynamic_slice_in_dim(conv_kernel, tensor_rank * channels, channels, 1).astype(
        jnp.float32
    )
    norm_scale = lax.dynamic_index_in_dim(norm_gains, section_index, 0, keepdims=False).astype(
        jnp.float32
    )
    head_gains = qk_gains.astype(jnp.float32)
    gathered_in, gathered_qkv = sent_together((conv_in, attn_qkv), ("section", "dp"), 0, 1)
    weights = (
        gathered_in.reshape(gathered_in.shape[0], -1),
        kernel,
        gathered_qkv,
        head_gains,
        mixer_out[0],
        gate_up[0, 0],
        gate_up[0, 1],
        down[0],
    )
    received = jnp.zeros(inputs.shape[2:], jnp.bfloat16)
    kept_states = []
    forward_out = []
    for step_number in range(micro_count + 1):
        micro_index = step_number - section_index
        in_range = (micro_index >= 0) & (micro_index < micro_count)
        segment_ids = lax.dynamic_index_in_dim(
            segments[0], jnp.clip(micro_index, 0, micro_count - 1), 0, keepdims=False
        )
        branch_index = jnp.where(in_range, section_index, 2)
        layer_in = jnp.where(
            first_section, inputs[0, min(step_number, micro_count - 1)], received
        ).astype(jnp.float32)
        result, saved = layer_forward(
            layer_in, norm_scale, segment_ids, branch_index, in_range, weights
        )
        result_low = result.astype(jnp.bfloat16)
        forward_out.append(result_low)
        kept_states.append(saved)
        if step_number < micro_count:
            received = passed_along(result_low, "section", 1)
    received_grad = jnp.zeros(inputs.shape[2:], jnp.bfloat16)
    backward_out = []
    section_totals = None
    pending_rows = []
    mixer_rows_all = []
    small_totals = None
    for step_number in range(micro_count + 1):
        micro_index = step_number - 1 + section_index
        in_range = (micro_index >= 0) & (micro_index < micro_count)
        segment_ids = lax.dynamic_index_in_dim(
            segments[0], jnp.clip(micro_index, 0, micro_count - 1), 0, keepdims=False
        )
        branch_index = jnp.where(in_range, section_index, 2)
        cotangent = out_cotangent[0, min(step_number, micro_count - 1)]
        grad_result = jnp.where(first_section, received_grad, cotangent).astype(
            jnp.float32
        ) * in_range.astype(jnp.float32)
        saved = jax.tree.map(
            lambda from_early, from_late: jnp.where(first_section, from_early, from_late),
            kept_states[max(step_number - 1, 0)],
            kept_states[min(step_number + 1, micro_count)],
        )
        grad_layer_in, section_rows, mixer_rows, small_parts = layer_backward(
            grad_result, saved, norm_scale, segment_ids, branch_index, in_range, weights
        )
        grad_low = grad_layer_in.astype(jnp.bfloat16)
        backward_out.append(grad_low)
        if step_number < micro_count:
            received_grad = passed_along(grad_low, "section", -1)
        pending_rows.append(section_rows)
        mixer_rows_all.append(mixer_rows)
        small_totals = accumulate(small_totals, small_parts)
    whole_parts = section_grads(pending_rows)
    section_totals = tuple(
        (
            part.astype(jnp.float32)
            for part in sum_packed(
                (
                    whole_parts[0].astype(jnp.bfloat16),
                    whole_parts[1].astype(jnp.bfloat16),
                    whole_parts[2].astype(jnp.bfloat16),
                ),
                "dp",
                (2, 2, 2),
            )
        )
    )
    grad_mixer_out, grad_gate_up, grad_down = section_totals
    normed_rows, grad_in_rows, grad_qkv_rows = join_rows(mixer_rows_all, 3)
    grad_in_total = product_left(normed_rows, grad_in_rows).reshape(gathered_in.shape)
    grad_qkv_total = product_left(normed_rows, grad_qkv_rows)
    grad_conv_in, grad_attn_qkv = sum_packed(
        (grad_in_total, grad_qkv_total), ("section", "dp"), (0, 0)
    )
    scales_full = jnp.where(
        jnp.arange(2)[:, None, None] == section_index, small_totals[0][None], 0.0
    )
    kernel_full = lax.dynamic_update_slice(
        jnp.zeros(conv_kernel.shape, jnp.float32), small_totals[1], (0, tensor_rank * channels)
    )
    grad_norm_gains, grad_conv_kernel, grad_qk_gains = (
        over_pieces(scales_full, ("section", "dp", "tensor")),
        over_pieces(kernel_full, ("section", "dp", "tensor")),
        over_pieces(small_totals[2], ("section", "dp", "tensor")),
    )
    activations = jnp.stack(
        [
            jnp.where(first_section, forward_out[micro_slot], forward_out[micro_slot + 1])
            for micro_slot in range(micro_count)
        ]
    )[None, None]
    input_grads = jnp.stack(
        [
            jnp.where(first_section, backward_out[micro_slot + 1], backward_out[micro_slot])
            for micro_slot in range(micro_count)
        ]
    )[None, None]
    return (
        activations,
        input_grads,
        grad_norm_gains,
        grad_conv_kernel,
        grad_qk_gains,
        grad_conv_in,
        grad_attn_qkv,
        grad_mixer_out,
        grad_gate_up,
        grad_down,
    )


def solution(mesh):
    in_specs = (
        P("dp", None, "tensor", None),
        P("dp", None, "tensor", None),
        P("dp", None, None),
        P(),
        P(),
        P(),
        P(("section", "dp"), None, "tensor"),
        P(("section", "dp"), "tensor"),
        P("section", "tensor", None),
        P("section", None, None, "tensor"),
        P("section", "tensor", None),
    )
    out_specs = (
        P("section", "dp", None, "tensor", None),
        P("section", "dp", None, "tensor", None),
        P(),
        P(),
        P(),
        P(("section", "dp"), None, "tensor"),
        P(("section", "dp"), "tensor"),
        P("section", "tensor", "dp"),
        P("section", None, "dp", "tensor"),
        P("section", "tensor", "dp"),
    )
    return jax.shard_map(local, mesh=mesh, in_specs=in_specs, out_specs=out_specs, check_vma=False)
```

profile of v0, /device:TPU:0, one launch (start us, length us, event | category | flops | bytes accessed | tf_op | source)
XLA Modules:
  0.0 1775.6 jit_solution(12545156093727271958)
XLA Ops:
  19.4 15.7 slice_bitcast_fusion.12
  35.0 65.2 %all-gather.6.cloned.1.call-done = bf16[1536,3584]{1,0:T(8,128)(2,1)} async-done(((bf16[24,3584]{1,0:T(8,128)(2,1)}), bf16[1536,3584]{1,0:T(8,128)(2,1)}) %all-gather.6.cloned.1.call-update) | async-done | bytes 11010064 | tf_op jit(solution)/shard_map/all_gather | solution.py:54
  131.5 17.9 %conditional.13 = (f32[128,3456]{1,0:T(8,128)}, f32[128,3456]{1,0:T(8,128)}, bf16[128,3456]{1,0:T(8,128)(2,1)}, bf16[128,1536]{1,0:T(8,128)(2,1)S(1)}) conditional(s32[]{:T(128)} %convert_element_type.439, () %tuple.140, (bf16[128,1536]{1,0:T(8,128)(2,1)S(1)}, bf16[1536,3456]{1,0:T(8,128)(2,1)}, bf16[1536,3456]{1,0:T(8,128)(2,1)}, ...), branch_computations={%region_10.11_spmd, %region_11.12_spmd} | conditional | flops 4079517696 | bytes 71958632 | solution.py:415
  166.5 10.1 conditional.14
  195.6 18.8 %conditional.15 = (f32[128,3456]{1,0:T(8,128)}, f32[128,3456]{1,0:T(8,128)}, bf16[128,3456]{1,0:T(8,128)(2,1)}, bf16[128,1536]{1,0:T(8,128)(2,1)}) conditional(s32[]{:T(128)} %convert_element_type.448, () %tuple.145, (bf16[128,1536]{1,0:T(8,128)(2,1)}, bf16[1536,3456]{1,0:T(8,128)(2,1)}, bf16[1536,3456]{1,0:T(8,128)(2,1)}, ...), branch_computations={%region_23.24_spmd, %region_24.25_spmd} | conditional | flops 4079517696 | bytes 73531520 | solution.py:415
  202.7 8.1 multiply_convert_fusion.1
  246.0 47.3 %collective-permute-start.1 = (bf16[64,1536]{1,0:T(8,128)(2,1)S(1)}, bf16[64,1536]{1,0:T(8,128)(2,1)S(1)}, u32[]{:S(2)}, u32[]{:S(2)}) collective-permute-start(bf16[64,1536]{1,0:T(8,128)(2,1)S(1)} %get-tuple-element.819), channel_id=1, source_target_pairs={{0,64},{1,65},{2,66},{3,67},{4,68},{5,69},{6,70},{7,71},{8,72},{9,... | collective-permute-start | bytes 589832 | tf_op jit(solution)/shard_map/ppermute | solution.py:62
  346.3 24.6 %conditional.20 = (bf16[128,1536]{1,0:T(8,128)(2,1)}, bf16[128,2,3456]{2,0,1:T(8,128)(2,1)}) conditional(s32[]{:T(128)} %convert_element_type.474, () %tuple.157, (bf16[128,1536]{1,0:T(8,128)(2,1)}, bf16[3456,1536]{1,0:T(8,128)(2,1)}, pred[]{:T(512)}, f32[128,3456]{1,0:T(8,128)}, f32[128,3456]{1,0:T(8,128)}, /*index=5*/f32[128,3456]{1,0:T(8,128)}, ...), branch_computations={%region_61.62_spmd, %region_62.63_spmd} | conditional | flops 4084776960 | bytes 97910888 | solution.py:455
  346.3 10.1 multiply_convert_fusion.6
  361.2 8.3 convolution_add_fusion.1
  384.9 8.4 conditional.21
  402.1 33.0 %collective-permute-done.3 = bf16[64,1536]{1,0:T(8,128)(2,1)S(1)} collective-permute-done((bf16[64,1536]{1,0:T(8,128)(2,1)S(1)}, bf16[64,1536]{1,0:T(8,128)(2,1)S(1)}, u32[]{:S(2)}, u32[]{:S(2)}) %collective-permute-start.3) | collective-permute-done | bytes 196640 | tf_op jit(solution)/shard_map/ppermute | solution.py:62
  440.1 24.6 %conditional.22 = (bf16[128,1536]{1,0:T(8,128)(2,1)}, bf16[128,2,3456]{2,0,1:T(8,128)(2,1)}) conditional(s32[]{:T(128)} %convert_element_type.484, () %tuple.162, (bf16[128,1536]{1,0:T(8,128)(2,1)}, bf16[3456,1536]{1,0:T(8,128)(2,1)}, pred[]{:T(512)}, f32[128,3456]{1,0:T(8,128)}, f32[128,3456]{1,0:T(8,128)}, /*index=5*/f32[128,3456]{1,0:T(8,128)}, ...), branch_computations={%region_82.83_spmd, %region_83.84_spmd} | conditional | flops 4084776960 | bytes 97910888 | solution.py:455
  440.1 10.1 multiply_convert_fusion.9
  454.9 8.3 convolution_add_fusion.2
  477.7 12.4 conditional.23
  501.2 9.8 convolution_convert_fusion.7
  511.0 24.6 %copy.184 = bf16[1,3456,32,48]{3,1,2,0:T(8,128)(2,1)} copy(bf16[1,3456,32,48]{1,3,2,0:T(8,128)(2,1)} %bitcast.606) | data formatting | bytes 21233664 | tf_op jit(solution)/shard_map/reshape | solution.py:35
  535.6 76.6 %reshape.1254 = bf16[32,165888]{1,0:T(8,128)(2,1)} reshape(bf16[32,1,3456,48]{3,2,0,1:T(8,128)(2,1)} %bitcast.576) | data formatting | bytes 21233664 | tf_op jit(solution)/shard_map/reshape | solution.py:68
  612.3 17.9 %convolution_convert_fusion.6 = bf16[2,3456,1536]{1,2,0:T(8,128)(2,1)} fusion(bf16[128,2,3456]{2,0,1:T(8,128)(2,1)} %get-tuple-element.561, bf16[128,2,3456]{2,0,1:T(8,128)(2,1)} %get-tuple-element.560, bf16[128,2,3456]{2,0,1:T(8,128)(2,1)} %get-tuple-element.559, bf16[128,1536]{0,1:T(8,128)(2,1)S(1)} %copy-done.86, bf16[128,1536]{0,1:T(8,128)(2,1)S(1)} %copy-done.87, ...), kind=kOutput, calls=%fused_computation.416 | convolution fusion | flops 8183808000 | bytes 27721728 | tf_op jit(solution)/shard_map/td,tkf->kdf/dot_general | solution.py:516
  630.1 18.3 %copy.310 = bf16[1,2,32,48,3456]{4,3,1,2,0:T(8,128)(2,1)} copy(bf16[1,2,32,48,3456]{4,3,2,1,0:T(8,128)(2,1)} %bitcast.578) | data formatting | bytes 42467328 | tf_op jit(solution)/shard_map/reshape | solution.py:35
  648.4 29.0 %reshape.1252 = bf16[32,331776]{1,0:T(8,128)(2,1)} reshape(bf16[32,1,2,48,3456]{4,3,2,0,1:T(8,128)(2,1)} %bitcast.577) | data formatting | bytes 42467328 | tf_op jit(solution)/shard_map/reshape | solution.py:68
  688.8 14.0 reshape.1250
  703.7 33.8 %pad_maximum_fusion.12 = bf16[32,534528]{1,0:T(8,128)(2,1)} fusion(bf16[32,165888]{1,0:T(8,128)(2,1)} %reshape.1254, bf16[32,331776]{1,0:T(8,128)(2,1)} %reshape.1252, bf16[32,36864]{1,0:T(8,128)(2,1)S(1)} %reshape.1250), kind=kLoop, calls=%fused_computation.414 | loop fusion | flops 102629376 | bytes 68419584 | tf_op jit(solution)/shard_map/concatenate | solution.py:68
  737.5 42.5 %reshape.1255 = bf16[133632,128]{1,0:T(8,128)(2,1)} reshape(bf16[32,534528]{1,0:T(8,128)(2,1)} %pad_maximum_fusion.12) | data formatting | bytes 68419584 | tf_op jit(solution)/shard_map/reshape | solution.py:70
  797.7 8.3 fusion.112
  806.0 12.8 reshape_reshape_reshape.3
  818.9 16.1 pad_maximum_fusion.13
  835.0 17.5 reshape.1246
  859.2 299.0 %all-gather.1 = f32[128,2,64]{2,1,0:T(2,128)S(1)} all-gather(f32[1,2,64]{2,1,0:T(2,128)S(1)} %add_bitcast_fusion), channel_id=2, replica_groups=mesh['section'=2,'dp'=32,'tensor'=2] {'section','dp','tensor'}, dimensions={0}, use_global_device_ids=true | all-gather | bytes 66048 | tf_op jit(solution)/shard_map/all_gather | solution.py:80
  1166.7 354.4 %all-reduce.72.cloned.1.call-done = bf16[133632,128]{1,0:T(8,128)(2,1)} async-done(((bf16[133632,128]{1,0:T(8,128)(2,1)}), bf16[133632,128]{1,0:T(8,128)(2,1)}) %all-reduce.72.cloned.1.call-update) | async-done | bytes 34209808
  1528.7 236.9 %reduce-scatter.2.cloned.1.call-done = f32[672,128]{1,0:T(8,128)} async-done(((f32[43008,128]{1,0:T(8,128)}), f32[672,128]{1,0:T(8,128)}) %reduce-scatter.2.cloned.1.call-update) | async-done | bytes 344080 | tf_op jit(solution)/shard_map/reduce_scatter | solution.py:71
  (503 shorter events, 356.9 us)
Async XLA Ops:
  7.2 93.0 %all-gather.6.cloned.1.call-start = ((), (), s32[]{:S(2)}) async-start(), calls=%async_computation.25 | async-start | bytes 11182080 | tf_op jit(solution)/shard_map/all_gather | solution.py:54
  10.4 489.9 %copy-start.69 = (f32[1536]{0:T(1024)}, f32[1536]{0:T(1024)S(1)}, u32[]{:S(2)}) copy-start(f32[1536]{0:T(1024)S(1)} %get-tuple-element.785) | copy-start | bytes 18436
  13.4 93.3 %all-to-all-start = ((bf16[2,64,1536]{2,1,0:T(8,128)(2,1)}), bf16[2,64,1536]{2,1,0:T(8,128)(2,1)}, u32[]{:S(2)}, u32[]{:S(2)}) async-start(bf16[2,64,1536]{2,1,0:T(8,128)(2,1)} %broadcast_in_dim.193), calls=%async_computation | async-start | bytes 786432 | tf_op jit(solution)/shard_map/all_to_all | solution.py:26
  155.3 6.0 collective-permute-start
  189.5 24.9 %all-to-all-start.12 = ((bf16[2,64,1536]{2,1,0:T(8,128)(2,1)}), bf16[2,64,1536]{2,1,0:T(8,128)(2,1)}, u32[]{:S(2)}, u32[]{:S(2)}) async-start(bf16[2,64,1536]{2,1,0:T(8,128)(2,1)} %broadcast_in_dim.205), calls=%async_computation.12 | async-start | bytes 786432 | tf_op jit(solution)/shard_map/all_to_all | solution.py:26
  216.6 5.1 all-to-all-start.13
  230.4 8.9 all-to-all-start.7
  239.3 58.8 %copy-start.22 = (bf16[1,2,64,1536]{3,2,1,0:T(8,128)(2,1)S(1)}, bf16[1,2,64,1536]{3,2,1,0:T(8,128)(2,1)}, u32[]{:S(2)}) copy-start(bf16[1,2,64,1536]{3,2,1,0:T(8,128)(2,1)} %param.41) | copy-start | bytes 1179652
  239.3 55.3 %all-to-all-start.15 = ((bf16[2,64,1536]{2,1,0:T(8,128)(2,1)}), bf16[2,64,1536]{2,1,0:T(8,128)(2,1)S(1)}, u32[]{:S(2)}, u32[]{:S(2)}) async-start(bf16[2,64,1536]{2,1,0:T(8,128)(2,1)} %bitcast.156), calls=%async_computation.15 | async-start | bytes 786432 | tf_op jit(solution)/shard_map/all_to_all | solution.py:41
  242.9 917.4 %all-gather.10.cloned.1.call-start = ((), (), s32[]{:S(2)}) async-start(), calls=%async_computation.27 | async-start | bytes 3170304 | tf_op jit(solution)/shard_map/all_gather | solution.py:80
  246.0 52.1 %collective-permute-start.1 = (bf16[64,1536]{1,0:T(8,128)(2,1)S(1)}, bf16[64,1536]{1,0:T(8,128)(2,1)S(1)}, u32[]{:S(2)}, u32[]{:S(2)}) collective-permute-start(bf16[64,1536]{1,0:T(8,128)(2,1)S(1)} %get-tuple-element.819), channel_id=1, source_target_pairs={{0,64},{1,65},{2,66},{3,67},{4,68},{5,69},{6,70},{7,71},{8,72},{9,... | collective-permute-start | bytes 589832 | tf_op jit(solution)/shard_map/ppermute | solution.py:62
  321.3 19.0 %collective-permute-start.2 = (bf16[64,1536]{1,0:T(8,128)(2,1)}, bf16[64,1536]{1,0:T(8,128)(2,1)}, u32[]{:S(2)}, u32[]{:S(2)}) collective-permute-start(bf16[64,1536]{1,0:T(8,128)(2,1)} %add_convert_fusion.26), channel_id=1, source_target_pairs={{64,0},{65,1},{66,2},{67,3},{68,4},{69,5},{70,6},{71,7},{72,8},{73... | collective-permute-start | bytes 589832 | tf_op jit(solution)/shard_map/ppermute | solution.py:62
  400.3 34.9 %collective-permute-start.3 = (bf16[64,1536]{1,0:T(8,128)(2,1)S(1)}, bf16[64,1536]{1,0:T(8,128)(2,1)S(1)}, u32[]{:S(2)}, u32[]{:S(2)}) collective-permute-start(bf16[64,1536]{1,0:T(8,128)(2,1)S(1)} %get-tuple-element.809), channel_id=1, source_target_pairs={{64,0},{65,1},{66,2},{67,3},{68,4},{69,5},{70,6},{71,7},{72,8},{73... | collective-permute-start | bytes 589832 | tf_op jit(solution)/shard_map/ppermute | solution.py:62
  495.2 5.1 all-to-all-start.23
  498.6 664.7 %all-gather.8.cloned.1.call-start = ((), (), s32[]{:S(2)}) async-start(), calls=%async_computation.26 | async-start | bytes 3170304 | tf_op jit(solution)/shard_map/all_gather | solution.py:80
  535.6 76.7 %copy-start.85 = (bf16[128,1536]{0,1:T(8,128)(2,1)S(1)}, bf16[128,1536]{0,1:T(8,128)(2,1)}, u32[]{:S(2)}) copy-start(bf16[128,1536]{0,1:T(8,128)(2,1)} %get-tuple-element.944) | copy-start | bytes 1179652
  535.6 76.7 %copy-start.86 = (bf16[128,1536]{0,1:T(8,128)(2,1)S(1)}, bf16[128,1536]{0,1:T(8,128)(2,1)}, u32[]{:S(2)}) copy-start(bf16[128,1536]{0,1:T(8,128)(2,1)} %get-tuple-element.945) | copy-start | bytes 1179652
  535.6 76.7 %copy-start.87 = (bf16[128,1536]{0,1:T(8,128)(2,1)S(1)}, bf16[128,1536]{0,1:T(8,128)(2,1)}, u32[]{:S(2)}) copy-start(bf16[128,1536]{0,1:T(8,128)(2,1)} %get-tuple-element.946) | copy-start | bytes 1179652
  703.7 817.5 %all-reduce.72.cloned.1.call-start = ((), (), s32[]{:S(2)}) async-start(), calls=%async_computation.29 | async-start | bytes 68419584
  780.1 985.5 %reduce-scatter.2.cloned.1.call-start = ((), (), s32[]{:S(2)}) async-start(), calls=%async_computation.28 | async-start | bytes 22364160 | tf_op jit(solution)/shard_map/reduce_scatter | solution.py:71
  852.5 306.4 %copy-start.174 = (f32[64]{0:T(128)S(1)}, f32[64]{0:T(128)}, u32[]{:S(2)}) copy-start(f32[64]{0:T(128)} %get-tuple-element.773) | copy-start | bytes 772
  852.5 306.4 %copy-start.19 = (bf16[64,1536]{1,0:T(8,128)(2,1)S(1)}, bf16[64,1536]{1,0:T(8,128)(2,1)}, u32[]{:S(2)}) copy-start(bf16[64,1536]{1,0:T(8,128)(2,1)} %copy-done.16) | copy-start | bytes 589828
  852.5 306.4 %copy-start.28 = (bf16[64,1536]{1,0:T(8,128)(2,1)S(1)}, bf16[64,1536]{1,0:T(8,128)(2,1)}, u32[]{:S(2)}) copy-start(bf16[64,1536]{1,0:T(8,128)(2,1)} %copy-done.24) | copy-start | bytes 589828
  852.6 306.4 %copy-start.34 = (f32[64,1536]{1,0:T(8,128)S(1)}, f32[64,1536]{1,0:T(8,128)}, u32[]{:S(2)}) copy-start(f32[64,1536]{1,0:T(8,128)} %copy-done.33) | copy-start | bytes 1179652
  852.6 306.4 %copy-start.59 = (f32[64,1536]{1,0:T(8,128)S(1)}, f32[64,1536]{1,0:T(8,128)}, u32[]{:S(2)}) copy-start(f32[64,1536]{1,0:T(8,128)} %copy-done.58) | copy-start | bytes 1179652
  852.6 306.4 %copy-start.68 = (f32[64,1536]{1,0:T(8,128)S(1)}, f32[64,1536]{1,0:T(8,128)}, u32[]{:S(2)}) copy-start(f32[64,1536]{1,0:T(8,128)} %get-tuple-element.811) | copy-start | bytes 1179652
  852.6 306.4 %copy-start.70 = (f32[1536]{0:T(1024)S(1)}, f32[1536]{0:T(1024)}, u32[]{:S(2)}) copy-start(f32[1536]{0:T(1024)} %copy-done.69) | copy-start | bytes 18436
  852.6 306.4 %copy-start.74 = (bf16[64,1536]{1,0:T(8,128)(2,1)S(1)}, bf16[64,1536]{1,0:T(8,128)(2,1)}, u32[]{:S(2)}) copy-start(bf16[64,1536]{1,0:T(8,128)(2,1)} %copy-done.73) | copy-start | bytes 589828
  852.6 306.4 %copy-start.77 = (bf16[64,1536]{1,0:T(8,128)(2,1)S(1)}, bf16[64,1536]{1,0:T(8,128)(2,1)}, u32[]{:S(2)}) copy-start(bf16[64,1536]{1,0:T(8,128)(2,1)} %copy-done.76) | copy-start | bytes 589828
  852.6 306.4 %copy-start.166 = (f32[64]{0:T(128)S(1)}, f32[64]{0:T(128)}, u32[]{:S(2)}) copy-start(f32[64]{0:T(128)} %copy-done.165) | copy-start | bytes 772
  852.7 306.6 %copy-start.72 = (bf16[1,64,1536]{2,1,0:T(8,128)(2,1)S(1)}, bf16[1,64,1536]{2,1,0:T(8,128)(2,1)}, u32[]{:S(2)}) copy-start(bf16[1,64,1536]{2,1,0:T(8,128)(2,1)} %get-tuple-element.818) | copy-start | bytes 589828
  852.7 306.6 %copy-start.75 = (bf16[1,64,1536]{2,1,0:T(8,128)(2,1)S(1)}, bf16[1,64,1536]{2,1,0:T(8,128)(2,1)}, u32[]{:S(2)}) copy-start(bf16[1,64,1536]{2,1,0:T(8,128)(2,1)} %get-tuple-element.808) | copy-start | bytes 589828
  (100 other events, 1026.1 us)
Sparse Core Ops, SparseCore 0:
  11.5 88.7 all-gather.5
  491.7 64.3 all-gather.9
  703.8 64.3 all-gather.7
  780.2 740.9 all-reduce.71
  1525.8 239.6 reduce-scatter.1
where the time goes:
time: 1790 us; the launch traced here: 1780 us
  waiting for transfers between devices  704 us (39%)
  blocking collectives  381 us (21%)
  local copies, waits for them, and re-layouts  325 us (18%)
  matrix products  148 us (8%)
  other arithmetic  121 us (7%)
  starting transfers between devices  74.4 us (4%)
    unnamed x6, waiting for transfers between devices  355 us
    all_gather x1, blocking collectives, over_pieces(): return lax.all_gather(shard, axis).sum(0)  299 us
    reduce_scatter x1, waiting for transfers between devices, sum_packed(): lax.psum_scatter(lines, axis, tiled=True).reshape(-1)  237 us
    reshape x3, local copies, waits for them, and re-layouts, sum_packed(): lines = jnp.concatenate([b.reshape(length, -1) for b in tiles], axis=1)  120 us
    all_gather x1, waiting for transfers between devices, sent_together(): whole = lax.all_gather(both, axis, axis=dim, tiled=True)  65.2 us
    reshape x2, local copies, waits for them, and re-layouts, sum_packed(): jnp.pad(lines, ((0, 0), (0, span * 128 - lines.shape[1]))).reshape(-1, 128)  60 us
    dot_general x10, matrix products, product_right(): lax.dot_general(left, right, (((1,), (1,)), ((), ())), preferred_element_...  56.1 us
    ppermute x4, starting transfers between devices, passed_along(): return lax.ppermute(shard, axis, pairs)  51.2 us
  transfers between devices with their start and end apart: 15, of which 9 were waited for; matrix products, arithmetic and copies ran while one was open for 25% of the time, Pallas kernels for 0%

commit v1 on v0

v1 whole, which is shorter than its diff:
```python
import jax
import jax.numpy as jnp
from jax import lax
from jax.sharding import Mesh
from jax.sharding import PartitionSpec as P

HEADS = 24
KV_HEADS = 8
HEAD_DIM = 64
GROUP = HEADS // KV_HEADS

EPSILON = 1e-05
ROPE_BASE = 1000000.0
MASKED_SCORE = -1e30

F32 = jnp.float32
BF16 = jnp.bfloat16

PLANE = ("y", "z")
AXES = ("xh", "xl", "y", "z", "c")


def product(left, right):
    return jnp.dot(left, right, preferred_element_type=F32)


def product_left(left, right):
    return lax.dot_general(left, right, (((0,), (0,)), ((), ())), preferred_element_type=F32)


def product_right(left, right):
    return lax.dot_general(left, right, (((1,), (1,)), ((), ())), preferred_element_type=F32)


def swapped(shard, axis):
    return lax.ppermute(shard, axis, [(0, 1), (1, 0)])


def spread(own):
    micro, half, width = own.shape
    return lax.all_gather(own, "c", axis=1, tiled=True).reshape(micro * 2 * half, width)


def halves(full, core):
    tiles = full.reshape(2, 2, -1, full.shape[-1])
    mine = lax.dynamic_index_in_dim(tiles, core, 1, keepdims=False)
    other = lax.dynamic_index_in_dim(tiles, 1 - core, 1, keepdims=False)
    return mine, other


def collect(partial, core):
    mine, other = halves(partial, core)
    return mine + swapped(other.astype(BF16), "c").astype(F32)


def mean_last(values):
    return jnp.mean(values, axis=-1, keepdims=True)


def inverse_rms(values):
    return lax.rsqrt(mean_last(values * values) + EPSILON)


def normalize(values):
    return values * inverse_rms(values)


def norm_backward(grad, gain, values):
    inverse = inverse_rms(values)
    normed = values * inverse
    scaled = grad * gain
    grad_gain = jnp.sum(grad * normed, axis=(0, 1))
    return inverse * (scaled - normed * mean_last(scaled * normed)), grad_gain


def shift_rows(values, offset):
    pad = jnp.zeros((values.shape[0], offset, values.shape[2]), values.dtype)
    return jnp.concatenate([pad, values[:, :-offset]], axis=1)


def conv_gate(projected, kernel, segments):
    channels = kernel.shape[1]
    taps = kernel.shape[0]
    gate_before = projected[..., :channels]
    gate_after = projected[..., channels : 2 * channels]
    signal = projected[..., 2 * channels :]
    mixed = gate_before * signal
    total = kernel[taps - 1] * mixed
    for offset in range(1, taps):
        same = (segments[:, offset:] == segments[:, :-offset]).astype(mixed.dtype)
        same = jnp.pad(same, ((0, 0), (offset, 0)))
        total = total + kernel[taps - 1 - offset] * shift_rows(mixed, offset) * same[..., None]
    return gate_after * total


def rotary_tables(length):
    half = HEAD_DIM // 2
    exponent = jnp.arange(half, dtype=F32) * (2.0 / HEAD_DIM)
    frequency = jnp.exp(-exponent * jnp.log(ROPE_BASE))
    angles = jnp.arange(length, dtype=F32)[:, None] * frequency[None, :]
    return (jnp.cos(angles), jnp.sin(angles))


def rotate(values, cosine, sine):
    half = values.shape[-1] // 2
    first, second = values[..., :half], values[..., half:]
    shape = (1, cosine.shape[0]) + (1,) * (values.ndim - 3) + (half,)
    cosine, sine = cosine.reshape(shape), sine.reshape(shape)
    return jnp.concatenate([first * cosine - second * sine, second * cosine + first * sine], axis=-1)


def prepare_heads(head_inputs, head_gains):
    micro, length, width = head_inputs.shape
    key_heads = width // ((GROUP + 2) * HEAD_DIM)
    grouped = head_inputs.reshape(micro, length, key_heads, GROUP + 2, HEAD_DIM)
    cosine, sine = rotary_tables(length)
    queries = rotate(normalize(grouped[:, :, :, :GROUP]) * head_gains[0], cosine, sine)
    keys = rotate(normalize(grouped[:, :, :, GROUP]) * head_gains[1], cosine, sine)
    return (queries, keys, grouped[:, :, :, GROUP + 1])


def einsum(spec, left, right):
    return jnp.einsum(spec, left, right, preferred_element_type=F32)


def attention_forward(head_inputs, head_gains, segments):
    micro, length, _ = head_inputs.shape
    queries, keys, values = [a.astype(BF16) for a in prepare_heads(head_inputs, head_gains)]
    scores = einsum("mtgjd,msgd->mgjts", queries, keys) * HEAD_DIM ** (-0.5)
    position = jnp.arange(length)
    allowed = (position[:, None] >= position[None, :]) & (
        segments[:, :, None] == segments[:, None, :]
    )
    scores = jnp.where(allowed[:, None, None], scores, MASKED_SCORE)
    terms = jnp.exp(scores - jnp.max(scores, axis=-1, keepdims=True))
    weights = terms / jnp.sum(terms, axis=-1, keepdims=True)
    attended = einsum("mgjts,msgd->mtgjd", weights.astype(BF16), values)
    return attended.reshape(micro, length, -1).astype(BF16), (queries, keys, values, weights)


def attention_backward(grad_attended, saved, head_inputs, head_gains):
    queries, keys, values, weights = saved
    grad_low = grad_attended.reshape(queries.shape).astype(BF16)
    grad_values = einsum("mgjts,mtgjd->msgd", weights.astype(BF16), grad_low)
    grad_weights = einsum("mtgjd,msgd->mgjts", grad_low, values)
    grad_scores = (
        weights * (grad_weights - jnp.sum(grad_weights * weights, axis=-1, keepdims=True))
    ).astype(BF16)
    scale = HEAD_DIM ** (-0.5)
    grad_queries = einsum("mgjts,msgd->mtgjd", grad_scores, keys) * scale
    grad_keys = einsum("mgjts,mtgjd->msgd", grad_scores, queries) * scale
    rebuild = jax.vjp(prepare_heads, head_inputs, head_gains)[1]
    return rebuild((grad_queries, grad_keys, grad_values))


def ffn_forward(inner, weight_gate, weight_up):
    gate = product(inner, weight_gate)
    up = product(inner, weight_up)
    return gate, up, (jax.nn.silu(gate) * up).astype(BF16)


def ffn_grads(grad_active, gate, up):
    sigmoid = jax.nn.sigmoid(gate)
    grad_gate = grad_active * up * sigmoid * (1.0 + gate * (1.0 - sigmoid))
    grad_up = grad_active * gate * sigmoid
    return grad_gate.astype(BF16), grad_up.astype(BF16)


def local(
    inputs,
    out_cotangent,
    segments,
    norm_gains,
    conv_kernel,
    qk_gains,
    conv_in,
    attn_qkv,
    mixer_out,
    gate_up,
    down,
):
    section = lax.axis_index("xh")
    first = section == 0
    core = lax.axis_index("c")
    place = lax.axis_index("y") * 4 + lax.axis_index("z")
    xl = lax.axis_index("xl")
    plane = lax.axis_size("y") * lax.axis_size("z")

    inputs, out_cotangent, segments = inputs[0], out_cotangent[0], segments[0]
    micro, half, width = inputs.shape
    length = 2 * half
    rows = micro * length
    channels = conv_in.shape[2]
    kernel = lax.dynamic_slice_in_dim(conv_kernel, core * channels, channels, 1).astype(F32)
    gains = lax.dynamic_index_in_dim(norm_gains, section, 0, keepdims=False).astype(F32)
    head_gains = qk_gains.astype(F32)
    weight_out, weight_gate, weight_up, weight_down = (
        mixer_out[0],
        gate_up[0, 0],
        gate_up[0, 1],
        down[0],
    )
    hidden_units = weight_down.shape[0]
    part = hidden_units // plane

    in_width = 3 * channels
    qkv_width = attn_qkv.shape[1]
    both = jnp.concatenate([conv_in.reshape(-1, in_width), attn_qkv], axis=1)
    whole = lax.all_gather(both, ("xh", "xl", "y", "z"), axis=0, tiled=True)
    weight_in, weight_qkv = whole[:, :in_width], whole[:, in_width:]

    part_gate = lax.dynamic_slice_in_dim(weight_gate, place * part, part, 1)
    part_up = lax.dynamic_slice_in_dim(weight_up, place * part, part, 1)
    part_down = lax.dynamic_slice_in_dim(weight_down, place * part, part, 0)

    def feed_forward(hidden):
        inner_own = (normalize(hidden) * gains[1]).astype(BF16)
        inner = spread(inner_own)
        gate, up, active = ffn_forward(inner, weight_gate, weight_up)
        return hidden + collect(product(active, weight_down), core), (inner_own, gate, up)

    def feed_forward_back(grad_low, grad, hidden, saved):
        _, gate, up = saved
        grad_active = product_right(spread(grad_low), weight_down)
        grad_gate, grad_up = ffn_grads(grad_active, gate, up)
        partial = product_right(grad_gate, weight_gate) + product_right(grad_up, weight_up)
        back, grad_gain = norm_backward(collect(partial, core), gains[1], hidden)
        grad_hidden = grad + back
        return grad_hidden, grad_gain

    def mixer_back(grad_hidden, grad_proj, weight, layer_in):
        partial = product_right(grad_proj, weight)
        back, grad_gain = norm_backward(collect(partial, core), gains[0], layer_in)
        return (grad_hidden + back).astype(BF16), grad_gain

    first_in = inputs.astype(F32)
    normed_own_0 = (normalize(first_in) * gains[0]).astype(BF16)
    projected = product(spread(normed_own_0), weight_in).reshape(micro, length, in_width)
    gated_0 = conv_gate(projected, kernel, segments).astype(BF16).reshape(rows, -1)
    hidden_0 = first_in + collect(product(gated_0, weight_out), core)
    result_0, ffn_0 = feed_forward(hidden_0)
    result_0 = result_0.astype(BF16)

    received = lax.ppermute(result_0, "xh", [(0, 1)])
    second_in = received.astype(F32)
    normed_own_1 = (normalize(second_in) * gains[0]).astype(BF16)
    head_inputs = product(spread(normed_own_1), weight_qkv).reshape(micro, length, qkv_width)
    gated_1, kept = attention_forward(head_inputs, head_gains, segments)
    gated_1 = gated_1.reshape(rows, -1)
    hidden_1 = second_in + collect(product(gated_1, weight_out), core)
    result_1, ffn_1 = feed_forward(hidden_1)
    result_1 = result_1.astype(BF16)

    def chosen(from_first, from_second):
        return jnp.where(first, from_first, from_second)

    def over_plane(own):
        return lax.all_gather(own, ("y", "z", "c")).reshape(-1, width)

    inner_all = over_plane(chosen(ffn_0[0], ffn_1[0]))
    normed_all = over_plane(chosen(normed_own_0, normed_own_1))
    gated = chosen(gated_0, gated_1)
    gated_all = lax.all_gather(gated, PLANE).reshape(plane * rows, -1)
    part_gates = ffn_forward(inner_all, part_gate, part_up)

    grad_hidden_1, gain_inner_1 = feed_forward_back(
        out_cotangent, out_cotangent.astype(F32), hidden_1, ffn_1
    )
    grad_mix_1 = spread(grad_hidden_1.astype(BF16))
    grad_gated_1 = product_right(grad_mix_1, weight_out).reshape(micro, length, -1)
    grad_heads_in, grad_head_gains = attention_backward(grad_gated_1, kept, head_inputs, head_gains)
    grad_proj_1 = grad_heads_in.astype(BF16).reshape(rows, -1)
    input_grad_1, gain_outer_1 = mixer_back(grad_hidden_1, grad_proj_1, weight_qkv, second_in)

    cotangent = lax.ppermute(input_grad_1, "xh", [(1, 0)])
    grad_all = over_plane(chosen(cotangent, out_cotangent))
    grad_hidden_0, gain_inner_0 = feed_forward_back(
        cotangent, cotangent.astype(F32), hidden_0, ffn_0
    )
    grad_mix_0 = spread(grad_hidden_0.astype(BF16))
    grad_gated_0 = product_right(grad_mix_0, weight_out).reshape(micro, length, -1)
    rebuild = jax.vjp(lambda p, k: conv_gate(p, k, segments), projected, kernel)[1]
    grad_projected, grad_kernel = rebuild(grad_gated_0)
    grad_proj_0 = grad_projected.astype(BF16).reshape(rows, -1)
    input_grad_0, gain_outer_0 = mixer_back(grad_hidden_0, grad_proj_0, weight_in, first_in)

    def from_plane(tiles):
        return lax.all_to_all(tiles, PLANE, 0, 0, tiled=True)

    def by_core(full):
        tiles = full.reshape(micro, 2, half, -1)
        return jnp.swapaxes(tiles, 0, 1).reshape(rows, -1)

    gate_all, up_all, active_all = part_gates
    grad_active_all = product_right(grad_all, part_down)
    grad_gate_all, grad_up_all = ffn_grads(grad_active_all, gate_all, up_all)
    parts = jnp.stack(
        [
            product_left(inner_all, grad_gate_all),
            product_left(inner_all, grad_up_all),
            product_left(grad_all, active_all),
        ]
    ).reshape(3, 2, plane, width // (2 * plane), part)

    def summed_over_pair(tiles, dim):
        mine = lax.dynamic_index_in_dim(tiles, xl, dim, keepdims=False)
        other = lax.dynamic_index_in_dim(tiles, 1 - xl, dim, keepdims=False)
        return mine + swapped(other.astype(BF16), "xl").astype(F32)

    mine = summed_over_pair(parts, 1).astype(BF16)
    arrived = from_plane(jnp.moveaxis(mine, 1, 0))
    lines = jnp.moveaxis(arrived, 0, 2).reshape(3, width // (2 * plane), hidden_units).astype(F32)
    grad_gate_up = lines[:2][None]
    grad_down = lines[2].T[None]

    grad_mix = by_core(chosen(grad_mix_0, grad_mix_1))
    tiles = grad_mix.reshape(rows, 2, plane, -1)
    columns = from_plane(jnp.moveaxis(tiles, 2, 0)).reshape(plane * rows, -1)
    gated_rows = gated_all.reshape(plane, micro, 2, half, -1)
    gated_rows = jnp.swapaxes(gated_rows, 1, 2).reshape(plane * rows, -1)
    out_parts = product_left(columns, gated_rows).reshape(2, -1, channels)
    grad_mixer_out = summed_over_pair(out_parts, 0).T[None]

    spare = in_width - qkv_width
    grad_proj = chosen(grad_proj_0, jnp.pad(grad_proj_1, ((0, 0), (0, spare))))
    tiles = jnp.moveaxis(by_core(grad_proj).reshape(rows, plane, -1), 1, 0)
    columns = from_plane(tiles).reshape(plane * rows, -1)
    in_parts = product_left(normed_all, columns)
    in_parts = in_parts.reshape(2, 2, plane, -1, in_width // plane)
    mine = summed_over_pair(in_parts, 1).astype(BF16)
    arrived = from_plane(jnp.moveaxis(mine, 1, 0))
    lines = jnp.moveaxis(arrived, 0, 2).reshape(2, -1, in_width)
    kept_lines = lax.dynamic_index_in_dim(lines, section, 0, keepdims=False)
    sent_lines = lax.dynamic_index_in_dim(lines, 1 - section, 0, keepdims=False)
    come = swapped(sent_lines, "xh")
    grad_conv_in = chosen(kept_lines, come).astype(F32).reshape(conv_in.shape)
    grad_attn_qkv = chosen(come, kept_lines)[:, :qkv_width].astype(F32)

    full_kernel = lax.dynamic_update_slice(
        jnp.zeros(conv_kernel.shape, F32), grad_kernel, (0, core * channels)
    )
    small = jnp.concatenate(
        [
            chosen(gain_outer_0, gain_outer_1),
            chosen(gain_inner_0, gain_inner_1),
            full_kernel.reshape(-1),
            grad_head_gains.reshape(-1),
        ]
    )
    count = small.shape[0]
    small = jnp.pad(small, (0, -count % 1024)).reshape(-1, 128)
    small = lax.all_gather(small, "c").sum(0)
    small = small + swapped(small, "xl")
    for axis in PLANE:
        copies = jnp.broadcast_to(small, (4, *small.shape))
        small = lax.all_to_all(copies, axis, 0, 0, tiled=True).sum(0)
    come = swapped(small, "xh")
    pair = [chosen(small, come).reshape(-1), chosen(come, small).reshape(-1)]
    grad_norm_gains = jnp.stack([a[: 2 * width].reshape(2, width) for a in pair])
    grad_conv_kernel = pair[0][2 * width : 5 * width].reshape(conv_kernel.shape)
    grad_qk_gains = pair[1][5 * width : count].reshape(qk_gains.shape)

    activations = chosen(result_0, result_1)[None, None]
    input_grads = chosen(input_grad_0, input_grad_1)[None, None]
    return (
        activations,
        input_grads,
        grad_norm_gains,
        grad_conv_kernel,
        grad_qk_gains,
        grad_conv_in,
        grad_attn_qkv,
        grad_mixer_out,
        grad_gate_up,
        grad_down,
    )


def solution(mesh):
    wide = Mesh(mesh.devices.reshape(2, 2, 4, 4, 2), AXES)
    dp = ("xl", "y", "z")
    everyone = ("xh", "xl", "y", "z")
    in_specs = (
        P(dp, None, "c", None),
        P(dp, None, "c", None),
        P(dp, None, None),
        P(),
        P(),
        P(),
        P(everyone, None, "c"),
        P(everyone, "c"),
        P("xh", "c", None),
        P("xh", None, None, "c"),
        P("xh", "c", None),
    )
    out_specs = (
        P("xh", dp, None, "c", None),
        P("xh", dp, None, "c", None),
        P(),
        P(),
        P(),
        P(everyone, None, "c"),
        P(everyone, "c"),
        P("xh", "c", dp),
        P("xh", None, dp, "c"),
        P("xh", "c", dp),
    )
    return jax.shard_map(local, mesh=wide, in_specs=in_specs, out_specs=out_specs, check_vma=False)
```

time: 1790 us -> 636 us (0.36)
  waiting for transfers between devices: 704 us -> 150 us
  blocking collectives: 381 us -> 23.1 us
  local copies, waits for them, and re-layouts: 325 us -> 150 us
  other arithmetic: 121 us -> 54.1 us
  matrix products: 148 us -> 184 us
  starting transfers between devices: 74.4 us -> 48.6 us
    unnamed x6 -> x5, waiting for transfers between devices: 355 us -> 0.75 us
    all_gather x1 -> x9, blocking collectives: 299 us -> 23.1 us  [the longest x8 21.2 us: spread(): lax.all_gather(own, 'c', axis=1, tiled=True)]
    reduce_scatter x1 -> x0, waiting for transfers between devices: 237 us -> none  [sum_packed(): lax.psum_scatter(lines, axis, tiled=True).reshape(-1)]
    reshape x22 -> x13, local copies, waits for them, and re-layouts: 232 us -> 55.8 us  [the longest x3 48.3 us: over_plane(): return lax.all_gather(own, ('y', 'z', 'c')).reshape(-1, width)]
    all_to_all x18 -> x0, blocking collectives: 82.2 us -> none  [the longest x10 46.5 us: from_everyone(): return lax.all_to_all(copies, axis, split_axis=0, concat_axis=0, tiled=True)]
    concatenate x7 -> x1, other arithmetic: 51.7 us -> 1.51 us  [local(): both = jnp.concatenate([conv_in.reshape(-1, in_width), attn_qkv], axis=1)]
    another operation x34 -> x4, local copies, waits for them, and re-layouts: 42.4 us -> 5.49 us  [the longest x1 4.47 us: local(): tiles = jnp.moveaxis(by_core(grad_proj).reshape(rows, plane, -1), 1, 0)]
    ppermute x4 -> x16, starting transfers between devices: 51.2 us -> 15.8 us  [the longest x14 8.88 us: swapped(): return lax.ppermute(shard, axis, [(0, 1), (1, 0)])]
  transfers between devices with their start and end apart: 15 -> 27, of which waited for: 9 -> 14; matrix products, arithmetic and copies ran while one was open for 25% -> 49% of each run, Pallas kernels for 0% -> 0%
where the time goes in v1:
time: 636 us; the launch traced here: 625 us
  matrix products  184 us (29%)
  local copies, waits for them, and re-layouts  150 us (24%)
  waiting for transfers between devices  150 us (24%)
  other arithmetic  54.1 us (9%)
  starting transfers between devices  48.6 us (8%)
  blocking collectives  23.1 us (4%)
  between operations  15.6 us (2%)
    all_gather x1, waiting for transfers between devices, local(): whole = lax.all_gather(both, ('xh', 'xl', 'y', 'z'), axis=0, tiled=True)  80.7 us
    dot_general x12, matrix products, product(): return jnp.dot(left, right, preferred_element_type=F32)  76 us
    dot_general x11, matrix products, product_right(): lax.dot_general(left, right, (((1,), (1,)), ((), ())), preferred_element_...  70.3 us
    reshape x3, local copies, waits for them, and re-layouts, over_plane(): return lax.all_gather(own, ('y', 'z', 'c')).reshape(-1, width)  48.3 us
    all_to_all x4, waiting for transfers between devices, from_plane(): return lax.all_to_all(tiles, PLANE, 0, 0, tiled=True)  33.5 us
    dot_general x5, matrix products, product_left(): lax.dot_general(left, right, (((0,), (0,)), ((), ())), preferred_element_...  30.7 us
    all_to_all x4, starting transfers between devices, from_plane(): return lax.all_to_all(tiles, PLANE, 0, 0, tiled=True)  24.3 us
    all_gather x8, blocking collectives, spread(): lax.all_gather(own, 'c', axis=1, tiled=True)  21.2 us
  transfers between devices with their start and end apart: 27, of which 14 were waited for; matrix products, arithmetic and copies ran while one was open for 49% of the time, Pallas kernels for 0%

profile of v1, /device:TPU:0, one launch (start us, length us, event | category | flops | bytes accessed | tf_op | source)
XLA Modules:
  0.0 625.4 jit_solution(9286986305645944644)
XLA Ops:
  19.5 80.7 %all-gather.10.cloned.1.call-done = bf16[1536,3584]{1,0:T(8,128)(2,1)} async-done(((bf16[24,3584]{1,0:T(8,128)(2,1)}), bf16[1536,3584]{1,0:T(8,128)(2,1)}) %all-gather.10.cloned.1.call-update) | async-done | bytes 11010064 | tf_op jit(solution)/shard_map/all_gather | solution.py:209
  116.0 9.0 %fusion.23 = f32[256,3456]{1,0:T(8,128)} fusion(bf16[256,1536]{1,0:T(8,128)(2,1)S(1)} %bitcast.533, bf16[1,2,1536,3456]{3,2,1,0:T(8,128)(2,1)} %param.20), kind=kOutput, calls=%fused_computation.23 | convolution fusion | flops 2717908992 | bytes 14942208 | tf_op jit(solution)/shard_map/dot_general | solution.py:24
  126.1 6.4 %multiply_convert_fusion.8 = (bf16[256,3456]{1,0:T(8,128)(2,1)}, f32[256,3456]{1,0:T(8,128)}) fusion(f32[256,3456]{1,0:T(8,128)} %fusion.23, bf16[256,1536]{1,0:T(8,128)(2,1)S(1)} %bitcast.534, bf16[1,2,1536,3456]{3,2,1,0:T(8,128)(2,1)S(1)} %bitcast.489), kind=kOutput, calls=%fused_computation.44 | convolution fusion | flops 2723217408 | bytes 20250624 | tf_op jit(solution)/shard_map/dot_general | solution.py:24
  132.6 6.3 %fusion.3 = f32[2,2,64,1536]{3,2,1,0:T(8,128)S(1)} fusion(bf16[2,2,64,3456]{3,2,1,0:T(8,128)(2,1)} %bitcast.549, bf16[1,3456,1536]{2,1,0:T(8,128)(2,1)} %param.21), kind=kOutput, calls=%fused_computation.3 | convolution fusion | flops 2717908992 | bytes 13959168 | tf_op jit(solution)/shard_map/dot_general | solution.py:24
  155.2 6.3 %copy.149 = bf16[1280,1536]{1,0:T(8,128)(2,1)} copy(bf16[1280,1536]{0,1:T(8,128)(2,1)} %slice_bitcast_fusion) | data formatting | bytes 7864320 | tf_op jit(solution)/shard_map/dot_general | solution.py:24
  201.7 9.1 %fusion.7 = f32[256,3456]{1,0:T(8,128)} fusion(bf16[256,1536]{1,0:T(8,128)(2,1)S(1)} %bitcast.537, bf16[1,3456,1536]{2,1,0:T(8,128)(2,1)} %param.21), kind=kOutput, calls=%fused_computation.7 | convolution fusion | flops 2717908992 | bytes 14942208 | tf_op jit(solution)/shard_map/dot_general | solution.py:32
  213.6 9.1 %fusion.21 = f32[256,3456]{1,0:T(8,128)} fusion(bf16[256,1536]{1,0:T(8,128)(2,1)S(1)} %bitcast.535, bf16[1,2,1536,3456]{3,2,1,0:T(8,128)(2,1)} %param.20), kind=kOutput, calls=%fused_computation.21 | convolution fusion | flops 2717908992 | bytes 14942208 | tf_op jit(solution)/shard_map/dot_general | solution.py:24
  222.7 6.5 %multiply_convert_fusion.7 = (bf16[256,3456]{1,0:T(8,128)(2,1)}, f32[256,3456]{1,0:T(8,128)}) fusion(f32[256,3456]{1,0:T(8,128)} %fusion.21, bf16[256,1536]{1,0:T(8,128)(2,1)S(1)} %bitcast.536, bf16[1,2,1536,3456]{3,2,1,0:T(8,128)(2,1)S(1)} %bitcast.491), kind=kOutput, calls=%fused_computation.42 | convolution fusion | flops 2723217408 | bytes 20250624 | tf_op jit(solution)/shard_map/dot_general | solution.py:24
  229.2 8.9 %fusion.11 = f32[256,1536]{1,0:T(8,128)S(1)} fusion(f32[256,3456]{1,0:T(8,128)} %fusion.7, f32[256,3456]{1,0:T(8,128)} %fusion.21, bf16[1,2,1536,3456]{3,2,1,0:T(8,128)(2,1)} %param.20), kind=kOutput, calls=%fused_computation.11 | convolution fusion | flops 2723217408 | bytes 19267584 | tf_op jit(solution)/shard_map/dot_general | solution.py:32
  238.2 10.8 %fusion.34 = f32[256,1536]{1,0:T(8,128)S(1)} fusion(f32[256,1536]{1,0:T(8,128)S(1)} %fusion.11, f32[256,3456]{1,0:T(8,128)} %fusion.21, f32[256,3456]{1,0:T(8,128)} %fusion.7, f32[256,3456]{1,0:T(8,128)} %get-tuple-element.115, bf16[1,2,1536,3456]{3,2,1,0:T(8,128)(2,1)} %param.20), kind=kOutput, calls=%fused_computation.48 | convolution fusion | flops 2727149568 | bytes 24379392 | tf_op jit(solution)/shard_map/dot_general | solution.py:32
  276.8 13.3 %collective-permute-done.7 = bf16[2,64,1536]{2,1,0:T(8,128)(2,1)S(1)} collective-permute-done((bf16[2,64,1536]{2,1,0:T(8,128)(2,1)S(1)}, bf16[2,64,1536]{2,1,0:T(8,128)(2,1)S(1)}, u32[]{:S(2)}, u32[]{:S(2)}) %collective-permute-start.7) | collective-permute-done | bytes 393248 | tf_op jit(solution)/shard_map/ppermute | solution.py:275
  294.8 6.3 %fusion.5 = f32[256,3456]{1,0:T(8,128)S(1)} fusion(bf16[256,1536]{1,0:T(8,128)(2,1)S(1)} %bitcast.538, bf16[1,3456,1536]{2,1,0:T(8,128)(2,1)} %param.21), kind=kOutput, calls=%fused_computation.5 | convolution fusion | flops 2717908992 | bytes 14942208 | tf_op jit(solution)/shard_map/dot_general | solution.py:32
  301.1 8.0 %fusion.9 = f32[256,1536]{1,0:T(8,128)S(1)} fusion(f32[256,3456]{1,0:T(8,128)S(1)} %fusion.5, f32[256,3456]{1,0:T(8,128)S(1)} %copy-done.97, bf16[1,2,1536,3456]{3,2,1,0:T(8,128)(2,1)} %param.20), kind=kOutput, calls=%fused_computation.9 | convolution fusion | flops 2723217408 | bytes 19267584 | tf_op jit(solution)/shard_map/dot_general | solution.py:32
  309.1 10.8 %fusion.37 = f32[256,1536]{1,0:T(8,128)S(1)} fusion(f32[256,1536]{1,0:T(8,128)S(1)} %fusion.9, f32[256,3456]{1,0:T(8,128)} %fusion.23, f32[256,3456]{1,0:T(8,128)} %copy-done.96, f32[256,3456]{1,0:T(8,128)} %get-tuple-element.109, bf16[1,2,1536,3456]{3,2,1,0:T(8,128)(2,1)} %param.20), kind=kOutput, calls=%fused_computation.49 | convolution fusion | flops 2727149568 | bytes 24379392 | tf_op jit(solution)/shard_map/dot_general | solution.py:32
  348.2 15.8 %fusion.182 = (bf16[1,1,1536,3456]{3,2,1,0:T(8,128)(2,1)}, bf16[1,1,1536,3456]{3,2,1,0:T(8,128)(2,1)}) fusion(bf16[1,2,1536,3456]{3,2,1,0:T(8,128)(2,1)} %param.20), kind=kLoop, calls=%fused_computation.324 | loop fusion | bytes 42467328 | tf_op jit(solution)/shard_map/slice | solution.py:199
  401.5 7.8 %all-to-all-done.4 = bf16[16,256,2,48]{1,3,2,0:T(8,128)(2,1)} async-done(((bf16[16,256,2,48]{1,3,2,0:T(8,128)(2,1)}), bf16[16,256,2,48]{1,3,2,0:T(8,128)(2,1)}, u32[]{:S(2)}, u32[]{:S(2)}) %all-to-all-start.4) | async-done | bytes 786464 | tf_op jit(solution)/shard_map/all_to_all | solution.py:288
  423.8 14.4 %all-to-all-done.2 = bf16[16,256,144]{1,2,0:T(8,128)(2,1)S(1)} async-done(((bf16[16,256,144]{1,2,0:T(8,128)(2,1)}), bf16[16,256,144]{1,2,0:T(8,128)(2,1)S(1)}, u32[]{:S(2)}, u32[]{:S(2)}) %all-to-all-start.2) | async-done | bytes 1179680 | tf_op jit(solution)/shard_map/all_to_all | solution.py:288
  439.1 6.5 %copy.178 = bf16[16,2,2,64,768]{4,3,2,1,0:T(8,128)(2,1)} copy(bf16[16,2,2,64,768]{4,3,1,2,0:T(8,128)(2,1)} %bitcast.509) | data formatting | bytes 12582912 | tf_op jit(solution)/shard_map/transpose | solution.py:320
  445.6 16.3 %copy.163 = bf16[4096,1536]{0,1:T(8,128)(2,1)} copy(bf16[4096,1536]{1,0:T(8,128)(2,1)} %bitcast.496) | data formatting | bytes 25165824 | tf_op jit(solution)/shard_map/reshape | solution.py:258
  461.9 6.4 %fusion.84 = f32[2,2,16,24,144]{4,3,2,1,0:T(8,128)S(1)} fusion(bf16[2,2,16,24,4096]{4,3,2,1,0:T(8,128)(2,1)} %bitcast.507, bf16[4096,144,1,1,1]{0,1,2,3,4:T(8,128)(2,1)S(1)} %reshape.495), kind=kOutput, calls=%fused_computation.106 | convolution fusion | flops 1811939328 | bytes 14647296 | tf_op jit(solution)/shard_map/dot_general | solution.py:28
  472.2 16.1 %copy.179 = bf16[4096,1536]{0,1:T(8,128)(2,1)} copy(bf16[4096,1536]{1,0:T(8,128)(2,1)} %bitcast.497) | data formatting | bytes 25165824 | tf_op jit(solution)/shard_map/reshape | solution.py:258
  488.3 10.8 %fusion.109 = f32[4096,216]{0,1:T(8,128)} fusion(bf16[4096,1536]{1,0:T(8,128)(2,1)} %bitcast.498, bf16[1,1,1536,3456]{3,2,1,0:T(8,128)(2,1)} %get-tuple-element.91, s32[]{:T(128)S(6)} %select_n.181), kind=kOutput, calls=%fused_computation.144 | convolution fusion | flops 2717908992 | bytes 16908292 | tf_op jit(solution)/shard_map/dot_general | solution.py:24
  499.1 10.8 %fusion.107 = f32[4096,216]{0,1:T(8,128)} fusion(bf16[4096,1536]{1,0:T(8,128)(2,1)} %bitcast.499, bf16[1,1,1536,3456]{3,2,1,0:T(8,128)(2,1)} %get-tuple-element.90, s32[]{:T(128)S(6)} %select_n.181), kind=kOutput, calls=%fused_computation.142 | convolution fusion | flops 2717908992 | bytes 16908292 | tf_op jit(solution)/shard_map/dot_general | solution.py:24
  509.9 15.8 %copy.180 = bf16[4096,1536]{0,1:T(8,128)(2,1)} copy(bf16[4096,1536]{1,0:T(8,128)(2,1)} %bitcast.500) | data formatting | bytes 25165824 | tf_op jit(solution)/shard_map/reshape | solution.py:258
  525.7 7.1 %fusion.119 = f32[4096,216]{0,1:T(8,128)S(1)} fusion(bf16[4096,1536]{1,0:T(8,128)(2,1)} %bitcast.501, bf16[1,3456,1536]{2,1,0:T(8,128)(2,1)} %param.21, s32[]{:T(128)S(6)} %select_n.181), kind=kOutput, calls=%fused_computation.191 | convolution fusion | flops 2717908992 | bytes 16785412 | tf_op jit(solution)/shard_map/dot_general | solution.py:32
  532.9 7.2 %fusion.64 = f32[1,2,16,48,216]{4,3,2,1,0:T(8,128)S(1)} fusion(bf16[2,16,48,4096]{3,2,1,0:T(8,128)(2,1)} %bitcast.502, f32[4096,216]{0,1:T(8,128)S(1)} %copy-done.95, f32[4096,216]{0,1:T(8,128)S(1)} %fusion.119), kind=kOutput, calls=%fused_computation.79 | convolution fusion | flops 2723217408 | bytes 20987904 | tf_op jit(solution)/shard_map/dot_general | solution.py:28
  540.1 7.1 %fusion.61 = f32[1,2,16,48,216]{4,3,2,1,0:T(8,128)S(1)} fusion(bf16[2,16,48,4096]{3,2,1,0:T(8,128)(2,1)S(1)} %bitcast.505, f32[4096,216]{0,1:T(8,128)} %fusion.107, f32[4096,216]{0,1:T(8,128)S(1)} %fusion.119, f32[4096,216]{0,1:T(8,128)} %fusion.109), kind=kOutput, calls=%fused_computation.78 | convolution fusion | flops 2726756352 | bytes 24526848 | tf_op jit(solution)/shard_map/dot_general | solution.py:28
  547.2 8.8 %fusion.67 = f32[1,2,16,48,216]{4,3,2,1,0:T(8,128)S(1)} fusion(bf16[2,16,48,4096]{3,2,1,0:T(8,128)(2,1)} %bitcast.506, f32[4096,216]{0,1:T(8,128)} %fusion.109, f32[4096,216]{0,1:T(8,128)} %fusion.107), kind=kOutput, calls=%fused_computation.80 | convolution fusion | flops 2723217408 | bytes 20987904 | tf_op jit(solution)/shard_map/dot_general | solution.py:28
  563.0 6.8 %all-to-all-start.3 = ((bf16[16,2,24,144]{3,2,1,0:T(8,128)(2,1)}), bf16[16,2,24,144]{3,2,1,0:T(8,128)(2,1)S(1)}, u32[]{:S(2)}, u32[]{:S(2)}) async-start(bf16[16,2,24,144]{3,2,1,0:T(8,128)(2,1)} %copy.170), calls=%async_computation.3 | async-start | bytes 786432 | tf_op jit(solution)/shard_map/all_to_all | solution.py:288
  569.8 10.5 %collective-permute-done.14 = bf16[48,768]{1,0:T(8,128)(2,1)S(1)} collective-permute-done((bf16[48,768]{1,0:T(8,128)(2,1)S(1)}, bf16[48,768]{1,0:T(8,128)(2,1)S(1)}, u32[]{:S(2)}, u32[]{:S(2)}) %collective-permute-start.14) | collective-permute-done | bytes 73760 | tf_op jit(solution)/shard_map/ppermute | solution.py:36
  585.5 9.0 %all-to-all-start.5 = ((bf16[16,3,48,216]{3,2,1,0:T(8,128)(2,1)}), bf16[16,3,48,216]{3,2,1,0:T(8,128)(2,1)S(1)}, u32[]{:S(2)}, u32[]{:S(2)}) async-start(bf16[16,3,48,216]{3,2,1,0:T(8,128)(2,1)} %copy.181), calls=%async_computation.5 | async-start | bytes 2359296 | tf_op jit(solution)/shard_map/all_to_all | solution.py:288
  596.8 11.3 %all-to-all-done.5 = bf16[16,3,48,216]{3,2,1,0:T(8,128)(2,1)S(1)} async-done(((bf16[16,3,48,216]{3,2,1,0:T(8,128)(2,1)}), bf16[16,3,48,216]{3,2,1,0:T(8,128)(2,1)S(1)}, u32[]{:S(2)}, u32[]{:S(2)}) %all-to-all-start.5) | async-done | bytes 995360 | tf_op jit(solution)/shard_map/all_to_all | solution.py:288
  (467 shorter events, 229.6 us)
Async XLA Ops:
  7.2 99.8 %copy-start = (bf16[1,768,1536]{2,1,0:T(8,128)(2,1)S(1)}, bf16[1,768,1536]{2,1,0:T(8,128)(2,1)}, u32[]{:S(2)}) copy-start(bf16[1,768,1536]{2,1,0:T(8,128)(2,1)} %param.19) | copy-start | bytes 7077892
  7.2 93.0 %all-gather.10.cloned.1.call-start = ((), (), s32[]{:S(2)}) async-start(), calls=%async_computation.6 | async-start | bytes 11182080 | tf_op jit(solution)/shard_map/all_gather | solution.py:209
  9.8 429.3 %all-gather.12.cloned.1.call-start = ((), (), s32[]{:S(2)}) async-start(), calls=%async_computation.7 | async-start | bytes 6684672 | tf_op jit(solution)/shard_map/all_gather | solution.py:263
  12.2 93.1 %copy-start.81 = (f32[2,128]{1,0:T(2,128)}, f32[2,128]{1,0:T(2,128)S(1)}, u32[]{:S(2)}) copy-start(f32[2,128]{1,0:T(2,128)S(1)} %get-tuple-element.118) | copy-start | bytes 3076
  12.9 92.4 %copy-start.61 = (f32[768]{0:T(1024)}, f32[768]{0:T(1024)S(1)}, u32[]{:S(2)}) copy-start(f32[768]{0:T(1024)S(1)} %get-tuple-element.65) | copy-start | bytes 9220
  12.9 92.4 %copy-start.63 = (f32[768]{0:T(1024)}, f32[768]{0:T(1024)S(1)}, u32[]{:S(2)}) copy-start(f32[768]{0:T(1024)S(1)} %get-tuple-element.66) | copy-start | bytes 9220
  12.9 92.4 %copy-start.65 = (f32[768]{0:T(1024)}, f32[768]{0:T(1024)S(1)}, u32[]{:S(2)}) copy-start(f32[768]{0:T(1024)S(1)} %get-tuple-element.64) | copy-start | bytes 9220
  109.1 2.1 collective-permute-start
  140.9 2.2 collective-permute-start.1
  145.2 18.2 %collective-permute-start.2 = (bf16[2,64,1536]{2,1,0:T(8,128)(2,1)}, bf16[2,64,1536]{2,1,0:T(8,128)(2,1)}, u32[]{:S(2)}, u32[]{:S(2)}) collective-permute-start(bf16[2,64,1536]{2,1,0:T(8,128)(2,1)} %fusion.115), channel_id=1, source_target_pairs={{0,64},{1,65},{2,66},{3,67},{4,68},{5,69},{6,70},{7,71},{8,72},{9,... | collective-permute-start | bytes 1179656 | tf_op jit(solution)/shard_map/ppermute | solution.py:244
  188.2 257.4 %all-gather.14.cloned.1.call-start = ((), (), s32[]{:S(2)}) async-start(), calls=%async_computation.8 | async-start | bytes 12976128 | tf_op jit(solution)/shard_map/all_gather | solution.py:258
  189.0 283.2 %all-gather.16.cloned.1.call-start = ((), (), s32[]{:S(2)}) async-start(), calls=%async_computation.9 | async-start | bytes 12976128 | tf_op jit(solution)/shard_map/all_gather | solution.py:258
  193.9 1.8 collective-permute-start.3
  199.0 310.9 %all-gather.18.cloned.1.call-start = ((), (), s32[]{:S(2)}) async-start(), calls=%async_computation.10 | async-start | bytes 12976128 | tf_op jit(solution)/shard_map/all_gather | solution.py:258
  249.0 1.8 collective-permute-start.5
  271.0 1.8 collective-permute-start.6
  275.5 14.6 %collective-permute-start.7 = (bf16[2,64,1536]{2,1,0:T(8,128)(2,1)S(1)}, bf16[2,64,1536]{2,1,0:T(8,128)(2,1)S(1)}, u32[]{:S(2)}, u32[]{:S(2)}) collective-permute-start(bf16[2,64,1536]{2,1,0:T(8,128)(2,1)S(1)} %fusion.93), channel_id=1, source_target_pairs={{64,0},{65,1},{66,2},{67,3},{68,4},{69,5},{70,6},{71,7},{72,8},{73... | collective-permute-start | bytes 1179656 | tf_op jit(solution)/shard_map/ppermute | solution.py:275
  320.0 8.8 %collective-permute-start.8 = (bf16[2,64,1536]{2,1,0:T(8,128)(2,1)S(1)}, bf16[2,64,1536]{2,1,0:T(8,128)(2,1)S(1)}, u32[]{:S(2)}, u32[]{:S(2)}) collective-permute-start(bf16[2,64,1536]{2,1,0:T(8,128)(2,1)S(1)} %fusion.131), channel_id=1, source_target_pairs={{0,1},{1,0},{2,3},{3,2},{4,5},{5,4},{6,7},{7,6},{8,9},{9,8},{10,11... | collective-permute-start | bytes 1179656 | tf_op jit(solution)/shard_map/ppermute | solution.py:36
  328.5 40.6 %collective-permute-start.4 = (bf16[2,64,1536]{2,1,0:T(8,128)(2,1)}, bf16[2,64,1536]{2,1,0:T(8,128)(2,1)}, u32[]{:S(2)}, u32[]{:S(2)}) collective-permute-start(bf16[2,64,1536]{2,1,0:T(8,128)(2,1)} %fusion.132), channel_id=1, source_target_pairs={{0,1},{1,0},{2,3},{3,2},{4,5},{5,4},{6,7},{7,6},{8,9},{9,8},{10,11... | collective-permute-start | bytes 1179656 | tf_op jit(solution)/shard_map/ppermute | solution.py:36
  341.7 1.9 collective-permute-start.9
  347.7 16.3 %collective-permute-start.10 = (f32[64,128]{1,0:T(8,128)S(1)}, f32[64,128]{1,0:T(8,128)S(1)}, u32[]{:S(2)}, u32[]{:S(2)}) collective-permute-start(f32[64,128]{1,0:T(8,128)S(1)} %reduce_sum.267), channel_id=1, source_target_pairs={{0,32},{32,0},{1,33},{33,1},{2,34},{34,2},{3,35},{35,3},{4,36},{36... | collective-permute-start | bytes 98312 | tf_op jit(solution)/shard_map/ppermute | solution.py:36
  364.7 11.1 %all-to-all-start = ((f32[4,64,128]{2,1,0:T(8,128)}), f32[4,64,128]{2,1,0:T(8,128)S(1)}, u32[]{:S(2)}, u32[]{:S(2)}) async-start(f32[4,64,128]{2,1,0:T(8,128)} %broadcast_in_dim.108), calls=%async_computation | async-start | bytes 262144 | tf_op jit(solution)/shard_map/all_to_all | solution.py:356
  376.5 10.1 %all-to-all-start.1 = ((f32[4,64,128]{2,1,0:T(8,128)}), f32[4,64,128]{2,1,0:T(8,128)}, u32[]{:S(2)}, u32[]{:S(2)}) async-start(f32[4,64,128]{2,1,0:T(8,128)} %broadcast_in_dim.109), calls=%async_computation.1 | async-start | bytes 262144 | tf_op jit(solution)/shard_map/all_to_all | solution.py:356
  386.6 22.7 %all-to-all-start.4 = ((bf16[16,256,2,48]{1,3,2,0:T(8,128)(2,1)}), bf16[16,256,2,48]{1,3,2,0:T(8,128)(2,1)}, u32[]{:S(2)}, u32[]{:S(2)}) async-start(bf16[16,256,2,48]{1,3,2,0:T(8,128)(2,1)} %copy.173), calls=%async_computation.4 | async-start | bytes 1572864 | tf_op jit(solution)/shard_map/all_to_all | solution.py:288
  409.3 28.9 %all-to-all-start.2 = ((bf16[16,256,144]{1,2,0:T(8,128)(2,1)}), bf16[16,256,144]{1,2,0:T(8,128)(2,1)S(1)}, u32[]{:S(2)}, u32[]{:S(2)}) async-start(bf16[16,256,144]{1,2,0:T(8,128)(2,1)} %copy.168), calls=%async_computation.2 | async-start | bytes 2359296 | tf_op jit(solution)/shard_map/all_to_all | solution.py:288
  414.4 5.5 collective-permute-start.11
  470.3 90.8 %collective-permute-start.12 = (bf16[2,16,24,144]{3,2,1,0:T(8,128)(2,1)}, bf16[2,16,24,144]{3,2,1,0:T(8,128)(2,1)}, u32[]{:S(2)}, u32[]{:S(2)}) collective-permute-start(bf16[2,16,24,144]{3,2,1,0:T(8,128)(2,1)} %fusion.122), channel_id=1, source_target_pairs={{0,32},{32,0},{1,33},{33,1},{2,34},{34,2},{3,35},{35,3},{4,36},{36... | collective-permute-start | bytes 663560 | tf_op jit(solution)/shard_map/ppermute | solution.py:36
  557.8 24.5 %collective-permute-start.15 = (bf16[3,16,48,216]{3,2,1,0:T(8,128)(2,1)}, bf16[3,16,48,216]{3,2,1,0:T(8,128)(2,1)S(1)}, u32[]{:S(2)}, u32[]{:S(2)}) collective-permute-start(bf16[3,16,48,216]{3,2,1,0:T(8,128)(2,1)} %fusion.82), channel_id=1, source_target_pairs={{0,32},{32,0},{1,33},{33,1},{2,34},{34,2},{3,35},{35,3},{4,36},{36... | collective-permute-start | bytes 2985992 | tf_op jit(solution)/shard_map/ppermute | solution.py:36
  559.6 20.8 %collective-permute-start.14 = (bf16[48,768]{1,0:T(8,128)(2,1)S(1)}, bf16[48,768]{1,0:T(8,128)(2,1)S(1)}, u32[]{:S(2)}, u32[]{:S(2)}) collective-permute-start(bf16[48,768]{1,0:T(8,128)(2,1)S(1)} %fusion.141), channel_id=1, source_target_pairs={{0,32},{32,0},{1,33},{33,1},{2,34},{34,2},{3,35},{35,3},{4,36},{36... | collective-permute-start | bytes 221192 | tf_op jit(solution)/shard_map/ppermute | solution.py:36
  563.0 18.0 %all-to-all-start.3 = ((bf16[16,2,24,144]{3,2,1,0:T(8,128)(2,1)}), bf16[16,2,24,144]{3,2,1,0:T(8,128)(2,1)S(1)}, u32[]{:S(2)}, u32[]{:S(2)}) async-start(bf16[16,2,24,144]{3,2,1,0:T(8,128)(2,1)} %copy.170), calls=%async_computation.3 | async-start | bytes 786432 | tf_op jit(solution)/shard_map/all_to_all | solution.py:288
  582.3 12.2 %collective-permute-start.13 = (bf16[24,2304]{1,0:T(8,128)(2,1)}, bf16[24,2304]{1,0:T(8,128)(2,1)}, u32[]{:S(2)}, u32[]{:S(2)}) collective-permute-start(bf16[24,2304]{1,0:T(8,128)(2,1)} %dynamic-slice_bitcast_fusion), channel_id=1, source_target_pairs={{0,64},{64,0},{1,65},{65,1},{2,66},{66,2},{3,67},{67,3},{4,68},{68... | collective-permute-start | bytes 331784 | tf_op jit(solution)/shard_map/ppermute | solution.py:36
  585.5 22.6 %all-to-all-start.5 = ((bf16[16,3,48,216]{3,2,1,0:T(8,128)(2,1)}), bf16[16,3,48,216]{3,2,1,0:T(8,128)(2,1)S(1)}, u32[]{:S(2)}, u32[]{:S(2)}) async-start(bf16[16,3,48,216]{3,2,1,0:T(8,128)(2,1)} %copy.181), calls=%async_computation.5 | async-start | bytes 2359296 | tf_op jit(solution)/shard_map/all_to_all | solution.py:288
  (114 other events, 782.3 us)
Sparse Core Ops, SparseCore 0:
  11.4 88.7 all-gather.9
  188.4 58.5 all-gather.11
  249.2 62.5 all-gather.13
  313.9 62.8 all-gather.15
  378.9 77.7 all-gather.17
